TPU v7x, 512 devices: a whole 4x8x8 slice. The times are simulated.
512 devices in a mesh: tenant: 32 (over z, x), tensor: 16 (over y, core).
Axes of the slice: x: 4, y: 8, z: 8, core: 2. Of those that a mesh axis runs over, the one named last changes fastest.
Arguments:
- activations: bfloat16 [1536, 8192], P('tenant', 'tensor'), may hold values from -6 to 6
- base_weight: bfloat16 [8192, 28672], P('tensor', 'tenant'), may hold values from -0.0625 to 0.0625
- v_codes: int32 [32, 8192, 256], P('tenant', 'tensor'), may hold values from 0 to 255, as said below
- u_codes: int32 [32, 256, 28672], P('tenant', 'tensor'), may hold values from 0 to 255, as said below
- group_bits: int32 [32, 8], P('tenant'), may hold values from 2 to 8, as said below
- v_scale: float32 [32, 256], P('tenant'), may hold values from 0.0055242716 to 0.044194173
- u_scale: float32 [32, 256], P('tenant', 'tensor'), may hold values from 0.015625 to 0.125
- tenant_of: int32 [1536, 1], replicated, may hold values from 0 to 19; in each aligned block of 1536 rows (0 to 1535, 1536 to 3071, ...) at most 96 rows name the same one
- owner_map: int32 [20], replicated, may hold values from 0 to 31, as said below
Outputs:
- projected: bfloat16 [1536, 28672], P('tensor', 'tenant')
Inputs may be any that keep to these rules, and one draw needn't show every extreme that they name: `tenant_of`: no tenant has more than 96 rows, some tenant has exactly 96, and every tenant has at least one row. `owner_map`: distinct owners for distinct tenants. `group_bits`: for each owner the first group has 8 bits, the next one to four groups 3 bits, the rest 2 bits. `v_codes`: A code of rank index r lies in 0 to 2 ** group_bits[o, r // 32] - 1. `u_codes`: A code of rank index r lies in 0 to 2 ** group_bits[o, r // 32] - 1.
All inputs are finite; a program needn't handle non-finite values.
Results may differ from a plain program's by a relative error of at most 0.03.
Values may be sent and summed in bfloat16 or wider, within the bound.
A program may use at most 128 MiB of HBM per device.

v0:
```python
import jax
import jax.numpy as jnp
from jax import lax
from jax.sharding import PartitionSpec as P

CAP = 96


def column_levels(bits_row, span_size, first_row, group_size):
    positions = first_row + jnp.arange(span_size, dtype=jnp.int32)
    group_ids = positions // group_size
    level_table = jnp.left_shift(jnp.ones_like(bits_row), bits_row)
    in_group = group_ids[:, None] == jnp.arange(bits_row.shape[0], dtype=jnp.int32)[None, :]
    return jnp.sum(jnp.where(in_group, level_table[None, :], 0), axis=1)


def dequantize(code_block, level_col, col_scale):
    spread = (level_col - 1).astype(jnp.float32)
    centered = 2.0 * code_block.astype(jnp.float32) - spread
    return (centered / spread * col_scale).astype(jnp.bfloat16)


def on_device(
    activations, base_weight, v_codes, u_codes, group_bits, v_scale, u_scale, tenant_of, owner_map
):
    owner_index = lax.axis_index("tenant")
    tensor_index = lax.axis_index("tensor")
    full_rank = v_codes.shape[2]
    rank_local = u_codes.shape[1]
    group_size = full_rank // group_bits.shape[1]
    tenant_ids = tenant_of[:, 0]
    row_total = tenant_ids.shape[0]
    tenant_total = owner_map.shape[0]
    member = (tenant_ids[:, None] == jnp.arange(tenant_total, dtype=jnp.int32)[None, :]).astype(
        jnp.int32
    )
    slot_index = jnp.sum(jnp.cumsum(member, axis=0) * member, axis=1) - 1
    row_owner = jnp.sum(member * owner_map[None, :], axis=1)
    gathered = lax.all_gather(activations, "tenant", axis=0, tiled=True)
    base_part = jnp.dot(gathered, base_weight, preferred_element_type=jnp.float32)
    owned_here = row_owner == owner_index
    targets = jnp.where(owned_here, slot_index, CAP)
    chosen_rows = (
        jnp.full((CAP,), row_total, jnp.int32)
        .at[targets]
        .set(jnp.arange(row_total, dtype=jnp.int32), mode="drop")
    )
    picked = jnp.take(gathered, chosen_rows, axis=0, mode="clip")
    v_levels = column_levels(group_bits[0], full_rank, 0, group_size)
    v_deq = dequantize(v_codes[0], v_levels[None, :], v_scale[0][None, :])
    rank_part = jnp.dot(picked, v_deq, preferred_element_type=jnp.float32)
    rank_code = lax.psum_scatter(
        rank_part.astype(jnp.bfloat16), "tensor", scatter_dimension=1, tiled=True
    )
    u_levels = column_levels(group_bits[0], rank_local, tensor_index * rank_local, group_size)
    u_deq = dequantize(u_codes[0], u_levels[:, None], u_scale[0][:, None])
    contrib = jnp.dot(rank_code, u_deq, preferred_element_type=jnp.float32)
    received = lax.all_to_all(
        contrib.astype(jnp.bfloat16), "tenant", split_axis=1, concat_axis=0, tiled=True
    ).astype(contrib.dtype)
    delta_rows = jnp.take(received, row_owner * CAP + slot_index, axis=0)
    return lax.psum_scatter(
        (base_part + delta_rows).astype(jnp.bfloat16), "tensor", scatter_dimension=0, tiled=True
    )


def solution(mesh):
    in_specs = (
        P("tenant", "tensor"),
        P("tensor", "tenant"),
        P("tenant", "tensor", None),
        P("tenant", "tensor", None),
        P("tenant", None),
        P("tenant", None),
        P("tenant", "tensor"),
        P(),
        P(),
    )
    out_specs = P("tensor", "tenant")
    return jax.shard_map(
        on_device, mesh=mesh, in_specs=in_specs, out_specs=out_specs, check_vma=False
    )
```

profile of v0, /device:TPU:1, one launch (start us, length us, event | category | flops | bytes accessed | tf_op | source)
XLA Modules:
  0.0 393.5 jit_solution(16745050118835021221)
XLA Ops:
  6.5 0.0 copy-start
  6.5 0.0 copy-start.4
  6.5 0.0 all-gather.2.cloned.1.call-start
  6.5 0.7 all-gather.2.cloned.1.call-update
  7.3 0.0 reduce-scatter.7.cloned.1.call-start
  7.3 0.7 reduce
  8.0 0.0 copy-start.2
  8.0 0.0 copy-start.3
  8.1 5.7 %reduce-window.6 = s32[20,12,128]{2,1,0:T(8,128)S(1)} reduce-window(s32[20,12,128]{2,1,0:T(8,128)S(1)} %fusion.12, s32[]{:T(128)} %constant.60.clone.1), window={size=1x1x128 pad=0_0x0_0x127_0}, to_apply=%region_1.2 | reduce-window | flops 3901440 | bytes 245764 | tf_op jit(solution)/shard_map/reduce-window
  13.8 0.1 slice.12
  13.9 0.2 copy.18
  14.1 0.1 copy.19
  14.2 0.1 broadcast_add_fusion
  14.3 0.1 copy.25
  14.4 0.8 fusion.13
  15.2 6.2 %scatter_custom_fusion = s32[96]{0:T(128)S(1)} fusion(s32[1536]{0:T(1024)S(1)} %fusion.14, s32[1536]{0:T(1024)S(1)} %iota.27, s32[]{:T(128)} %constant.65.clone.1), kind=kCustom, calls=%fused_computation.52 | custom fusion | bytes 388 | tf_op jit(solution)/shard_map/scatter | solution.py:46
  21.4 0.7 shift-left_bitcast_fusion
  22.1 0.1 select_reduce_fusion.2
  22.2 0.1 select_reduce_fusion.1
  22.3 73.3 %all-gather.2.cloned.1.call-done = bf16[1536,512]{1,0:T(8,128)(2,1)} async-done(((bf16[48,512]{1,0:T(8,128)(2,1)}), bf16[1536,512]{1,0:T(8,128)(2,1)}) %all-gather.2.cloned.1.call-update) | async-done | bytes 1572880 | tf_op jit(solution)/shard_map/all_gather | solution.py:39
  95.6 2.4 gather_fusion
  98.0 0.0 copy-done.4
  98.0 2.0 fusion.3
  100.0 0.0 reduce-scatter.7.cloned.1.call-update
  100.0 57.3 %reduce-scatter.7.cloned.1.call-done = bf16[16,96]{1,0:T(8,128)(2,1)} async-done(((bf16[256,96]{1,0:T(8,128)(2,1)}), bf16[16,96]{1,0:T(8,128)(2,1)}) %reduce-scatter.7.cloned.1.call-update) | async-done | bytes 3088
  157.3 0.0 copy-done.2
  157.3 0.0 copy-done.3
  157.3 2.3 convolution_convert_fusion
  159.6 2.8 copy.27
  162.5 9.1 %all-to-all-start = ((bf16[96,32,896]{2,0,1:T(8,128)(2,1)}), bf16[96,32,896]{2,0,1:T(8,128)(2,1)}, u32[]{:S(2)}, u32[]{:S(2)}) async-start(bf16[96,32,896]{2,0,1:T(8,128)(2,1)} %bitcast.49), calls=%async_computation | async-start | bytes 11010048 | tf_op jit(solution)/shard_map/all_to_all | solution.py:58
  171.6 0.0 reduce-scatter.5.cloned.1.call-start
  171.7 119.7 %all-to-all-done = bf16[96,32,896]{2,0,1:T(8,128)(2,1)} async-done(((bf16[96,32,896]{2,0,1:T(8,128)(2,1)}), bf16[96,32,896]{2,0,1:T(8,128)(2,1)}, u32[]{:S(2)}, u32[]{:S(2)}) %all-to-all-start) | async-done | bytes 5505056 | tf_op jit(solution)/shard_map/all_to_all | solution.py:58
  291.4 8.1 %convert_element_type.67 = f32[96,32,896]{2,0,1:T(8,128)} convert(bf16[96,32,896]{2,0,1:T(8,128)(2,1)} %all-to-all-done) | non-fusion elementwise | flops 2752512 | bytes 16515072 | tf_op jit(solution)/shard_map/convert_element_type | solution.py:60
  299.5 0.0 copy-start.1
  299.5 11.4 %gather_fusion.1 = f32[1536,896]{1,0:T(8,128)} fusion(f32[3072,896]{1,0:T(8,128)} %bitcast.48, s32[2048]{0:T(1024)S(1)} %pad_clamp_fusion), kind=kCustom, calls=%fused_computation.1 | custom fusion | bytes 11016192 | tf_op jit(solution)/shard_map/jit(_take)/gather | solution.py:61
  310.9 0.0 copy-done
  310.9 0.0 copy-done.1
  310.9 4.9 %add_convert_fusion = bf16[1536,896]{1,0:T(8,128)(2,1)} fusion(f32[1536,896]{1,0:T(8,128)} %gather_fusion.1, bf16[1536,512]{1,0:T(8,128)(2,1)S(1)} %copy-done.1, bf16[512,896]{1,0:T(8,128)(2,1)S(1)} %copy-done, pred[1536]{0:T(1024)(128)(4,1)S(1)} %get-tuple-element.7), kind=kOutput, calls=%fused_computation.5 | convolution fusion | flops 1413414912 | bytes 10749440 | tf_op jit(solution)/shard_map/dot_general | solution.py:40
  315.8 0.0 reduce-scatter.5.cloned.1.call-update
  315.8 71.1 %reduce-scatter.5.cloned.1.call-done = bf16[96,896]{1,0:T(8,128)(2,1)} async-done(((bf16[1536,896]{1,0:T(8,128)(2,1)}), bf16[96,896]{1,0:T(8,128)(2,1)}) %reduce-scatter.5.cloned.1.call-update) | async-done | bytes 172048 | tf_op jit(solution)/shard_map/reduce_scatter | solution.py:62
  (14 shorter events, 0.2 us)
Async XLA Ops:
  6.5 304.4 %copy-start = (bf16[512,896]{1,0:T(8,128)(2,1)S(1)}, bf16[512,896]{1,0:T(8,128)(2,1)}, u32[]{:S(2)}) copy-start(bf16[512,896]{1,0:T(8,128)(2,1)} %param.10) | copy-start | bytes 2752516
  6.5 91.5 %copy-start.4 = (f32[1,256]{1,0:T(1,128)S(1)}, f32[1,256]{1,0:T(1,128)}, u32[]{:S(2)}) copy-start(f32[1,256]{1,0:T(1,128)} %param.14) | copy-start | bytes 3076
  6.5 89.1 %all-gather.2.cloned.1.call-start = ((), (), s32[]{:S(2)}) async-start(), calls=%async_computation.3 | async-start | bytes 1622016 | tf_op jit(solution)/shard_map/all_gather | solution.py:39
  7.3 150.1 %reduce-scatter.7.cloned.1.call-start = ((), (), s32[]{:S(2)}) async-start(), calls=%async_computation.5 | async-start | bytes 69632
  8.0 149.3 %copy-start.2 = (s32[1,16,28672]{2,1,0:T(8,128)S(1)}, s32[1,16,28672]{2,1,0:T(8,128)}, u32[]{:S(2)}) copy-start(s32[1,16,28672]{2,1,0:T(8,128)} %param.12) | copy-start | bytes 5505028
  8.0 149.3 %copy-start.3 = (f32[1,16]{1,0:T(1,128)S(1)}, f32[1,16]{1,0:T(1,128)}, u32[]{:S(2)}) copy-start(f32[1,16]{1,0:T(1,128)} %param.15) | copy-start | bytes 196
  162.5 128.9 %all-to-all-start = ((bf16[96,32,896]{2,0,1:T(8,128)(2,1)}), bf16[96,32,896]{2,0,1:T(8,128)(2,1)}, u32[]{:S(2)}, u32[]{:S(2)}) async-start(bf16[96,32,896]{2,0,1:T(8,128)(2,1)} %bitcast.49), calls=%async_computation | async-start | bytes 11010048 | tf_op jit(solution)/shard_map/all_to_all | solution.py:58
  171.6 215.3 %reduce-scatter.5.cloned.1.call-start = ((), (), s32[]{:S(2)}) async-start(), calls=%async_computation.4 | async-start | bytes 2924544 | tf_op jit(solution)/shard_map/reduce_scatter | solution.py:62
  299.5 11.4 %copy-start.1 = (bf16[1536,512]{1,0:T(8,128)(2,1)S(1)}, bf16[1536,512]{1,0:T(8,128)(2,1)}, u32[]{:S(2)}) copy-start(bf16[1536,512]{1,0:T(8,128)(2,1)} %all-gather.2.cloned.1.call-done) | copy-start | bytes 4718596
Sparse Core Ops, SparseCore 0:
  10.5 85.0 all-gather.1
  100.1 57.1 reduce-scatter.6
  316.0 70.9 reduce-scatter.4
where the time goes:
time: 395 us; the launch traced here: 393 us
  waiting for transfers between devices  322 us (82%)
  local copies, waits for them, and re-layouts  23.4 us (6%)
  other arithmetic  16.3 us (4%)
  between operations  13.3 us (3%)
  starting transfers between devices  9.19 us (2%)
  matrix products  9.17 us (2%)
    all_to_all x1, waiting for transfers between devices, on_device(): lax.all_to_all(contrib.astype(jnp.bfloat16), 'tenant', split_axis=1, conc...  120 us
    all_gather x1, waiting for transfers between devices, on_device(): gathered = lax.all_gather(activations, 'tenant', axis=0, tiled=True)  73.3 us
    reduce_scatter x1, waiting for transfers between devices, on_device(): lax.psum_scatter((base_part + delta_rows).astype(jnp.bfloat16), 'tensor',...  71.1 us
    unnamed x4, waiting for transfers between devices  58 us
    gather x1, local copies, waits for them, and re-layouts, on_device(): delta_rows = jnp.take(received, row_owner * CAP + slot_index, axis=0)  11.4 us
    all_to_all x1, starting transfers between devices, on_device(): lax.all_to_all(contrib.astype(jnp.bfloat16), 'tenant', split_axis=1, conc...  9.1 us
    convert_element_type x1, other arithmetic, on_device(): received = lax.all_to_all(contrib.astype(jnp.bfloat16), 'tenant', split_a...  8.09 us
  transfers between devices with their start and end apart: 4, of which 4 were waited for; matrix products, arithmetic and copies ran while one was open for 4% of the time, Pallas kernels for 0%

commit v1 on v0

v1 whole, which is shorter than its diff:
```python
import functools

import jax
import jax.numpy as jnp
from jax import lax
from jax.experimental import pallas as pl
from jax.experimental.pallas import tpu as pltpu
from jax.sharding import PartitionSpec as P

MESH = pl.DeviceIdType.MESH
BF16, F32, I32 = jnp.bfloat16, jnp.float32, jnp.int32

NX, NC = 4, 2
SLOTS = 128
Z_ORDER = (0, -1, 1, -2, 2, -3, 3, -4)


def kernel(
    act, w_hbm, vc_hbm, uc_hbm, bits, v_scale, u_scale, tenant, owner_map, out,
    g, w, vc, uc, uq, vq, ur, rank_out, rank_in, code, codes, slot_hot, row_owner, slot_key,
    acc, sib_out, sib_in, ring_up, ring_dn,
    load_sem, a_send, a_recv, u_send, u_recv, r_send, r_recv, c_send, c_recv,
    x_send, x_recv, up_send, up_recv, dn_send, dn_recv,
    *, n_tenant, n_tensor,
):
    t, s = lax.axis_index("tenant"), lax.axis_index("tensor")
    nz, ny = n_tenant // NX, n_tensor // NC
    z, x = t // NX, t % NX
    y, c = s // NC, s % NC
    rows_t, depth = act.shape
    rows = g.shape[0]
    cols = w.shape[1]
    rank_local = uc.shape[0]
    full_rank = vc.shape[1]
    n_tenants = owner_map.shape[0]
    group = full_rank // bits.shape[1]
    rows_s = out.shape[0]

    def remote(src, dst, send_sem, recv_sem, device):
        return pltpu.make_async_remote_copy(
            src_ref=src, dst_ref=dst, send_sem=send_sem, recv_sem=recv_sem,
            device_id=device, device_id_type=MESH,
        )

    def wait_bytes(ref, sem):
        pltpu.make_async_copy(ref, ref, sem).wait()

    loads = [
        pltpu.make_async_copy(uc_hbm.at[0], uc, load_sem.at[0]),
        pltpu.make_async_copy(vc_hbm.at[0], vc, load_sem.at[1]),
        pltpu.make_async_copy(w_hbm, w, load_sem.at[2]),
        pltpu.make_async_copy(act, g.at[pl.ds(t * rows_t, rows_t)], load_sem.at[3]),
    ]
    for load in loads:
        load.start()

    barrier = pltpu.get_barrier_semaphore()

    def greet_tenant(i, carry):
        pl.semaphore_signal(barrier, 1, device_id=((t + i) % n_tenant, s), device_id_type=MESH)
        return carry

    def greet_tensor(i, carry):
        pl.semaphore_signal(barrier, 1, device_id=(t, (s + i) % n_tensor), device_id_type=MESH)
        return carry

    lax.fori_loop(1, n_tenant, greet_tenant, 0)
    lax.fori_loop(1, n_tensor, greet_tensor, 0)

    u_spread = (jnp.left_shift(1, bits[0, s * rank_local // group]) - 1).astype(F32)
    diagonal = lax.broadcasted_iota(I32, (rank_local, rank_local), 0) == lax.broadcasted_iota(
        I32, (rank_local, rank_local), 1
    )
    u_factor = (
        jnp.sum(jnp.where(diagonal, u_scale[...], 0.0), axis=1, keepdims=True) / u_spread
    )
    loads[0].wait()

    def dequantize_u(i, carry):
        block = uc[:, pl.ds(pl.multiple_of(i * cols, 128), cols)]
        uq[i] = ((2.0 * block.astype(F32) - u_spread) * u_factor).astype(BF16)
        return carry

    lax.fori_loop(0, n_tenant, dequantize_u, 0)

    pl.semaphore_wait(barrier, n_tenant + n_tensor - 2)

    def block_at(dz, dx):
        return ((z + dz + nz) % nz) * NX + (x + dx + NX) % NX

    up, dn, right, left = block_at(1, 0), block_at(-1, 0), block_at(0, 1), block_at(0, -1)

    def g_at(block):
        return g.at[pl.ds(block * rows_t, rows_t)]

    def send_block(block, to, src=None):
        remote(
            g_at(block) if src is None else src, g_at(block), a_send, a_recv.at[block], (to, s)
        ).start()

    def wait_block(block):
        wait_bytes(g_at(block), a_recv.at[block])

    def send_u(i, carry):
        to = (t + i) % n_tenant
        remote(uq.at[to], ur.at[pl.ds(t * rank_local, rank_local)], u_send, u_recv, (to, s)).start()
        return carry

    for to in (up, dn, right, left):
        send_block(t, to, act)

    def relay(j):
        if j % 2 == 0:
            block = block_at(Z_ORDER[j], -1)
            wait_block(block)
            send_block(block, right)
        else:
            block = block_at(Z_ORDER[j], 1)
            wait_block(block)
            send_block(block, left)

    lax.fori_loop(1, 4, send_u, 0)
    lane = lax.broadcasted_iota(I32, (1, full_rank), 1)
    v_spread = jnp.zeros((1, full_rank), F32)
    for i in range(bits.shape[1]):
        spread = (jnp.left_shift(1, bits[0, i]) - 1).astype(F32)
        v_spread = jnp.where(lane // group == i, spread, v_spread)
    v_factor = v_scale[...] / v_spread
    loads[1].wait()
    vq[...] = ((2.0 * vc[...].astype(F32) - v_spread) * v_factor).astype(BF16)

    for j in range(1, nz):
        dz = Z_ORDER[j]
        block = block_at(dz, 0)
        wait_block(block)
        if -4 < dz < 0:
            send_block(block, up)
        if 0 < dz < 3:
            send_block(block, dn)
        send_block(block, right)
        send_block(block, left)
        relay(j - 1)
        lax.fori_loop(4 * j, 4 * j + 4, send_u, 0)
    relay(nz - 1)

    tri = (
        lax.broadcasted_iota(I32, (128, 128), 0) <= lax.broadcasted_iota(I32, (128, 128), 1)
    ).astype(BF16)
    carry = jnp.zeros((32, 1), F32)
    for b in range(rows // 128):
        ids = tenant[:, b * 128:(b + 1) * 128]
        member = (lax.broadcasted_iota(I32, (32, 128), 0) == ids).astype(F32)
        count = carry + jnp.dot(member.astype(BF16), tri, preferred_element_type=F32)
        carry = count[:, 127:128]
        slot = jnp.sum(count * member, axis=0, keepdims=True) - 1.0
        owner = jnp.zeros((1, 128), F32)
        for i in range(n_tenants):
            owner = jnp.where(ids == i, owner_map[i].astype(F32), owner)
        key = owner * float(SLOTS) + slot
        slot_key[:, b * 128:(b + 1) * 128] = key.astype(I32)
        column = jnp.transpose(jnp.broadcast_to(key, (128, 128))).astype(I32)
        slot_hot[b * 128:(b + 1) * 128, :] = (
            column % SLOTS == lax.broadcasted_iota(I32, (128, 128), 1)
        ).astype(BF16)
        row_owner[b * 128:(b + 1) * 128, :] = column // SLOTS

    loads[3].wait()
    for j in range(nz):
        wait_block(block_at(Z_ORDER[j], 1 if j % 2 == 0 else -1))
        wait_block(block_at(Z_ORDER[j], 2))

    pick = (
        slot_key[...] == t * SLOTS + lax.broadcasted_iota(I32, (SLOTS, rows), 0)
    ).astype(BF16)
    picked = jnp.dot(pick, g[...], preferred_element_type=F32).astype(BF16)
    part = jnp.dot(picked, vq[...], preferred_element_type=F32)
    rank_out[...] = jnp.transpose(part).astype(BF16)

    def send_rank(i, carry):
        to = (s + i) % n_tensor
        remote(
            rank_out.at[pl.ds(to * rank_local, rank_local)],
            rank_in.at[pl.ds(s * rank_local, rank_local)],
            r_send, r_recv, (t, to),
        ).start()
        return carry

    lax.fori_loop(1, n_tensor, send_rank, 0)
    mine = pl.ds(pl.multiple_of(s * rank_local, rank_local), rank_local)
    rank_in[mine, :] = rank_out[mine, :]

    loads[2].wait()
    step = 2 * rows_s
    half = rows // step // 2

    def shared(i, carry):
        here = pl.ds(pl.multiple_of(i * step, step), step)
        acc[here, :] = jnp.dot(g[here, :], w[...], preferred_element_type=F32)
        return carry

    lax.fori_loop(0, half, shared, 0)

    wait_bytes(rank_in.at[pl.ds(0, (n_tensor - 1) * rank_local)], r_recv)
    total = jnp.zeros((rank_local, SLOTS), F32)
    for i in range(n_tensor):
        total = total + rank_in[i * rank_local:(i + 1) * rank_local, :].astype(F32)
    code[...] = total.astype(BF16)

    def send_code(i, carry):
        to = (t + i) % n_tenant
        remote(code, codes.at[pl.ds(t * rank_local, rank_local)], c_send, c_recv, (to, s)).start()
        return carry

    lax.fori_loop(1, n_tenant, send_code, 0)
    here_t = pl.ds(pl.multiple_of(t * rank_local, rank_local), rank_local)
    codes[here_t, :] = code[...]
    ur[here_t, :] = uq[t]

    lax.fori_loop(half, 2 * half, shared, 0)

    others = pl.ds(0, (n_tenant - 1) * rank_local)
    wait_bytes(codes.at[others], c_recv)
    wait_bytes(ur.at[others], u_recv)

    owner_lane = lax.broadcasted_iota(I32, (step, n_tenant * rank_local), 1) // rank_local

    def ring_block(j):
        away = (j // 2 + 1) * (1 - j // (ny - 1))
        return (y + (2 * (j % 2) - 1) * away + ny) % ny

    def terms(j, carry):
        d = ring_block(j)
        here = pl.ds(pl.multiple_of(d * step, step), step)
        spread_codes = lax.dot_general(
            slot_hot[here, :], codes[...], (((1,), (1,)), ((), ())), preferred_element_type=F32
        )
        owner = row_owner[here, :]
        owner = jnp.concatenate([owner] * (n_tenant * rank_local // 128), axis=1)
        spread_codes = jnp.where(owner == owner_lane, spread_codes, 0.0).astype(BF16)
        value = acc[here, :] + jnp.dot(spread_codes, ur[...], preferred_element_type=F32)
        acc[here, :] = value
        theirs = pl.ds(pl.multiple_of(d * step + (1 - c) * rows_s, rows_s), rows_s)
        sib_out[d] = acc[theirs, :].astype(BF16)
        remote(sib_out.at[d], sib_in.at[d], x_send, x_recv.at[d], (t, y * NC + 1 - c)).start()
        return carry

    lax.fori_loop(0, ny, terms, 0)

    piece = 16
    pieces = rows_s // 2 // piece
    y_up, y_dn = ((y + 1) % ny) * NC + c, ((y + ny - 1) % ny) * NC + c

    def chip_sum(d, first):
        here = pl.ds(pl.multiple_of(d * step + c * rows_s + first, piece), piece)
        return acc[here, :] + sib_in[d, first:first + piece, :].astype(F32)

    def ring_step(k, carry):
        for p in range(pieces):
            for way in range(2):
                d = (y + ny - 1 - k) % ny if way == 0 else (y + 1 + k) % ny
                first = (way * pieces + p) * piece
                slots, send, recv, to = (
                    (ring_up, up_send, up_recv, (t, y_up))
                    if way == 0
                    else (ring_dn, dn_send, dn_recv, (t, y_dn))
                )
                lines = pl.ds(p * piece, piece)
                wait_bytes(slots.at[k - 1, lines], recv.at[k - 1, p])
                slots[k - 1, lines, :] = (
                    slots[k - 1, lines, :].astype(F32) + chip_sum(d, first)
                ).astype(BF16)
                remote(
                    slots.at[k - 1, lines], slots.at[k, lines], send, recv.at[k, p], to
                ).start()
        return carry

    start_up, start_dn = (y + ny - 1) % ny, (y + 1) % ny
    wait_bytes(sib_in.at[start_up], x_recv.at[start_up])
    wait_bytes(sib_in.at[start_dn], x_recv.at[start_dn])
    for p in range(pieces):
        lines = pl.ds(p * piece, piece)
        ring_up[ny - 1, lines, :] = chip_sum(start_up, p * piece).astype(BF16)
        remote(
            ring_up.at[ny - 1, lines], ring_up.at[0, lines], up_send, up_recv.at[0, p], (t, y_up)
        ).start()
        ring_dn[ny - 1, lines, :] = chip_sum(start_dn, (pieces + p) * piece).astype(BF16)
        remote(
            ring_dn.at[ny - 1, lines], ring_dn.at[0, lines], dn_send, dn_recv.at[0, p], (t, y_dn)
        ).start()

    def wait_sibling(j, carry):
        d = ring_block(j)
        wait_bytes(sib_in.at[d], x_recv.at[d])
        return carry

    lax.fori_loop(2, ny, wait_sibling, 0)
    lax.fori_loop(1, ny - 1, ring_step, 0)
    for p in range(pieces):
        for way in range(2):
            slots, recv = (ring_up, up_recv) if way == 0 else (ring_dn, dn_recv)
            first = (way * pieces + p) * piece
            lines = pl.ds(p * piece, piece)
            wait_bytes(slots.at[ny - 2, lines], recv.at[ny - 2, p])
            out[first:first + piece, :] = (
                slots[ny - 2, lines, :].astype(F32) + chip_sum(y, first)
            ).astype(BF16)

    wait_bytes(g.at[pl.ds(0, (n_tenant - 1) * rows_t)], a_send)
    wait_bytes(ur.at[others], u_send)
    wait_bytes(rank_in.at[pl.ds(0, (n_tensor - 1) * rank_local)], r_send)
    wait_bytes(codes.at[others], c_send)
    wait_bytes(sib_out, x_send)
    wait_bytes(ring_up.at[pl.ds(0, ny - 1)], up_send)
    wait_bytes(ring_dn.at[pl.ds(0, ny - 1)], dn_send)


def on_device(
    n_tenant, n_tensor,
    activations, base_weight, v_codes, u_codes, group_bits, v_scale, u_scale, tenant_of, owner_map,
):
    rows_t, depth = activations.shape
    cols = base_weight.shape[1]
    rows = tenant_of.shape[0]
    full_rank = v_codes.shape[2]
    rank_local = u_codes.shape[1]
    rows_s = rows // n_tensor
    ny = n_tensor // NC
    all_ranks = n_tenant * rank_local
    vmem = pl.BlockSpec(memory_space=pltpu.VMEM)
    smem = pl.BlockSpec(memory_space=pltpu.SMEM)
    hbm = pl.BlockSpec(memory_space=pl.ANY)
    dma = pltpu.SemaphoreType.DMA
    pieces = rows_s // 2 // 16
    return pl.pallas_call(
        functools.partial(kernel, n_tenant=n_tenant, n_tensor=n_tensor),
        out_shape=jax.ShapeDtypeStruct((rows_s, cols), BF16),
        in_specs=[hbm, hbm, hbm, hbm, smem, vmem, vmem, vmem, smem],
        out_specs=vmem,
        scratch_shapes=[
            pltpu.VMEM((rows, depth), BF16),
            pltpu.VMEM((depth, cols), BF16),
            pltpu.VMEM((depth, full_rank), I32),
            pltpu.VMEM(u_codes.shape[1:], I32),
            pltpu.VMEM((n_tenant, rank_local, cols), BF16),
            pltpu.VMEM((depth, full_rank), BF16),
            pltpu.VMEM((all_ranks, cols), BF16),
            pltpu.VMEM((full_rank, SLOTS), BF16),
            pltpu.VMEM((full_rank, SLOTS), BF16),
            pltpu.VMEM((rank_local, SLOTS), BF16),
            pltpu.VMEM((all_ranks, SLOTS), BF16),
            pltpu.VMEM((rows, SLOTS), BF16),
            pltpu.VMEM((rows, 128), I32),
            pltpu.VMEM((1, rows), I32),
            pltpu.VMEM((rows, cols), F32),
            pltpu.VMEM((ny, rows_s, cols), BF16),
            pltpu.VMEM((ny, rows_s, cols), BF16),
            pltpu.VMEM((ny, rows_s // 2, cols), BF16),
            pltpu.VMEM((ny, rows_s // 2, cols), BF16),
            dma((4,)), dma, dma((n_tenant,)), dma, dma, dma, dma, dma, dma,
            dma, dma((ny,)), dma, dma((ny - 1, pieces)), dma, dma((ny - 1, pieces)),
        ],
        compiler_params=pltpu.CompilerParams(
            collective_id=0, has_side_effects=True, vmem_limit_bytes=48 * 1024 * 1024
        ),
        name="up_projection",
    )(
        activations, base_weight, v_codes, u_codes, group_bits, v_scale, u_scale,
        tenant_of.reshape(1, rows), owner_map,
    )


def solution(mesh):
    in_specs = (
        P("tenant", "tensor"),
        P("tensor", "tenant"),
        P("tenant", "tensor", None),
        P("tenant", "tensor", None),
        P("tenant", None),
        P("tenant", None),
        P("tenant", "tensor"),
        P(),
        P(),
    )
    return jax.shard_map(
        functools.partial(on_device, mesh.shape["tenant"], mesh.shape["tensor"]),
        mesh=mesh, in_specs=in_specs, out_specs=P("tensor", "tenant"), check_vma=False,
    )
```

time: 395 us -> 102 us (0.26)
  the two profiles are of different devices: /device:TPU:1 before, /device:TPU:8 now
where the time goes in v1:
time: 102 us
  Pallas kernels  93 us (91%)
  local copies, waits for them, and re-layouts  8.52 us (8%)
    pallas_call x1, Pallas kernels, on_device(): pl.pallas_call(functools.partial(kernel, n_tenant=n_tenant, n_tensor=n_te...  93 us
    unnamed x19, local copies, waits for them, and re-layouts  8.52 us

profile of v1, /device:TPU:8, one launch (start us, length us, event | category | flops | bytes accessed | tf_op | source)
XLA Modules:
  0.0 101.6 jit_solution(2028299252540403538)
XLA Ops:
  0.0 0.0 copy-start
  0.0 1.5 %copy-done = s32[1,16,28672]{2,1,0:T(8,128)S(1)} copy-done((s32[1,16,28672]{2,1,0:T(8,128)S(1)}, s32[1,16,28672]{2,1,0:T(8,128)}, u32[]{:S(2)}) %copy-start) | copy-done | bytes 1835032
  1.5 0.0 copy-start.1
  1.5 1.2 %copy-done.1 = bf16[512,896]{1,0:T(8,128)(2,1)S(1)} copy-done((bf16[512,896]{1,0:T(8,128)(2,1)S(1)}, bf16[512,896]{1,0:T(8,128)(2,1)}, u32[]{:S(2)}) %copy-start.1) | copy-done | bytes 917528
  2.7 0.0 copy-start.2
  2.7 1.0 %copy-done.2 = s32[1,512,256]{2,1,0:T(8,128)S(1)} copy-done((s32[1,512,256]{2,1,0:T(8,128)S(1)}, s32[1,512,256]{2,1,0:T(8,128)}, u32[]{:S(2)}) %copy-start.2) | copy-done | bytes 524312
  3.7 0.0 copy-start.3
  3.7 0.8 copy-done.3
  4.5 0.0 copy-start.4
  4.5 0.7 copy-done.4
  5.2 0.0 copy-start.5
  5.2 0.7 copy-done.5
  5.9 0.0 copy-start.6
  5.9 0.7 copy-done.6
  6.5 0.0 copy-start.7
  6.6 0.7 copy-done.7
  7.2 0.0 copy-start.8
  7.2 0.7 copy-done.8
  7.9 93.0 %up_projection.1 = bf16[96,896]{1,0:T(8,128)(2,1)S(1)} custom-call(bf16[48,512]{1,0:T(8,128)(2,1)S(1)} %copy-done.3, bf16[512,896]{1,0:T(8,128)(2,1)S(1)} %copy-done.1, s32[1,512,256]{2,1,0:T(8,128)S(1)} %copy-done.2, s32[1,16,28672]{2,1,0:T(8,128)S(1)} %copy-done, s32[1,8]{1,0:T(1,128)S(1)} %copy-done.6, f32[1,256]{1,0:T(1,128)S(1)} %copy-done.5, ...), custom_call_target="tpu_custom_call" | custom-call | tf_op jit(solution)/shard_map/up_projection/pallas_call | solution.py:334
  100.9 0.7 copy.11
Async XLA Ops:
  0.0 1.5 %copy-start = (s32[1,16,28672]{2,1,0:T(8,128)S(1)}, s32[1,16,28672]{2,1,0:T(8,128)}, u32[]{:S(2)}) copy-start(s32[1,16,28672]{2,1,0:T(8,128)} %uc_hbm.1) | copy-start | bytes 5505028
  1.5 1.2 %copy-start.1 = (bf16[512,896]{1,0:T(8,128)(2,1)S(1)}, bf16[512,896]{1,0:T(8,128)(2,1)}, u32[]{:S(2)}) copy-start(bf16[512,896]{1,0:T(8,128)(2,1)} %w_hbm.1) | copy-start | bytes 2752516
  2.7 1.0 %copy-start.2 = (s32[1,512,256]{2,1,0:T(8,128)S(1)}, s32[1,512,256]{2,1,0:T(8,128)}, u32[]{:S(2)}) copy-start(s32[1,512,256]{2,1,0:T(8,128)} %vc_hbm.1) | copy-start | bytes 1572868
  3.7 0.8 copy-start.3
  4.5 0.7 copy-start.4
  5.2 0.7 copy-start.5
  5.9 0.7 copy-start.6
  6.5 0.7 copy-start.7
  7.2 0.7 copy-start.8

commit v2 on v1

v2 whole, which is shorter than its diff:
```python
import functools

import jax
import jax.numpy as jnp
from jax import lax
from jax.experimental import pallas as pl
from jax.experimental.pallas import tpu as pltpu
from jax.sharding import PartitionSpec as P

MESH = pl.DeviceIdType.MESH
BF16, F32, I32 = jnp.bfloat16, jnp.float32, jnp.int32

NX, NC = 4, 2
SLOTS = 128
Z_ORDER = (0, -1, 1, -2, 2, -3, 3, -4)
RELAYED = 6
LAG = 3
PIECE = 16
Y_FAR_FIRST = (4, 3, -3, 2, -2, 1, -1)
T_FAR_FIRST = tuple(
    sorted(
        ((dz, dx) for dz in Z_ORDER for dx in (0, 1, -1, 2) if (dz, dx) != (0, 0)),
        key=lambda at: -abs(at[0]) - abs(at[1]),
    )
)


def kernel(
    act, w_hbm, vc_hbm, uc_hbm, bits, v_scale, u_scale, tenant, owner_map, out,
    g, w, vc, uc, uq, vq, ur, rank_out, rank_sib, rank_sum, rank_in, code, codes,
    slot_hot, row_owner, slot_key, acc, sib_out, sib_in, stage, ring_up, ring_dn,
    load_sem, a_send, a_recv, u_send, u_recv, q_send, q_recv, r_send, r_recv, c_send, c_recv,
    x_send, x_recv, up_send, up_recv, dn_send, dn_recv, token,
    *, n_tenant, n_tensor,
):
    t, s = lax.axis_index("tenant"), lax.axis_index("tensor")
    nz, ny = n_tenant // NX, n_tensor // NC
    z, x = t // NX, t % NX
    y, c = s // NC, s % NC
    rows_t, depth = act.shape
    rows = g.shape[0]
    cols = w.shape[1]
    rank_local = uc.shape[0]
    full_rank = vc.shape[1]
    n_tenants = owner_map.shape[0]
    group = full_rank // bits.shape[1]
    rows_s = out.shape[0]

    def remote(src, dst, send_sem, recv_sem, device):
        return pltpu.make_async_remote_copy(
            src_ref=src, dst_ref=dst, send_sem=send_sem, recv_sem=recv_sem,
            device_id=device, device_id_type=MESH,
        )

    def wait_bytes(ref, sem):
        pltpu.make_async_copy(ref, ref, sem).wait()

    def at_tenant(dz, dx):
        return ((z + dz + nz) % nz) * NX + (x + dx + NX) % NX

    def at_tensor(dy):
        return ((y + dy + ny) % ny) * NC + c

    up, dn, right, left = at_tenant(1, 0), at_tenant(-1, 0), at_tenant(0, 1), at_tenant(0, -1)
    y_up, y_dn, sibling = at_tensor(1), at_tensor(-1), y * NC + 1 - c

    loads = [
        pltpu.make_async_copy(uc_hbm.at[0], uc, load_sem.at[0]),
        pltpu.make_async_copy(vc_hbm.at[0], vc, load_sem.at[1]),
        pltpu.make_async_copy(w_hbm, w, load_sem.at[2]),
        pltpu.make_async_copy(act, g.at[pl.ds(t * rows_t, rows_t)], load_sem.at[3]),
    ]
    for load in loads:
        load.start()

    barrier = pltpu.get_barrier_semaphore()
    for device in (
        (up, s), (dn, s), (right, s), (left, s), (t, y_up), (t, y_dn), (t, sibling),
    ):
        pl.semaphore_signal(barrier, 1, device_id=device, device_id_type=MESH)

    u_spread = (jnp.left_shift(1, bits[0, s * rank_local // group]) - 1).astype(F32)
    diagonal = lax.broadcasted_iota(I32, (rank_local, rank_local), 0) == lax.broadcasted_iota(
        I32, (rank_local, rank_local), 1
    )
    u_factor = (
        jnp.sum(jnp.where(diagonal, u_scale[...], 0.0), axis=1, keepdims=True) / u_spread
    )
    loads[0].wait()

    def dequantize_u(i, carry):
        block = uc[:, pl.ds(pl.multiple_of(i * cols, 128), cols)]
        uq[i] = ((2.0 * block.astype(F32) - u_spread) * u_factor).astype(BF16)
        return carry

    lax.fori_loop(0, n_tenant, dequantize_u, 0)

    lane = lax.broadcasted_iota(I32, (1, full_rank), 1)
    v_spread = jnp.zeros((1, full_rank), F32)
    for i in range(bits.shape[1]):
        spread = (jnp.left_shift(1, bits[0, i]) - 1).astype(F32)
        v_spread = jnp.where(lane // group == i, spread, v_spread)
    v_factor = v_scale[...] / v_spread
    loads[1].wait()
    vq[...] = ((2.0 * vc[...].astype(F32) - v_spread) * v_factor).astype(BF16)
    loads[2].wait()
    loads[3].wait()

    pl.semaphore_wait(barrier, 7)

    def g_at(block):
        return g.at[pl.ds(block * rows_t, rows_t)]

    def send_block(block, to):
        remote(g_at(block), g_at(block), a_send, a_recv.at[block], (to, s)).start()

    def wait_block(block):
        wait_bytes(g_at(block), a_recv.at[block])

    def send_u(to):
        remote(uq.at[to], ur.at[pl.ds(t * rank_local, rank_local)], u_send, u_recv, (to, s)).start()

    def across(block, j):
        send_block(block, right)
        send_block(block, left)
        if j >= RELAYED:
            send_block(block, at_tenant(0, 2))

    def relay(j):
        if 0 <= j < RELAYED:
            block = at_tenant(Z_ORDER[j], -1 if j % 2 == 0 else 1)
            wait_block(block)
            send_block(block, right if j % 2 == 0 else left)
            send_u(block)

    def greet(i):
        for device in ((t, y_up), (t, y_dn)):
            pl.semaphore_signal(token.at[i], 1, device_id=device, device_id_type=MESH)

    send_block(t, up)
    send_block(t, dn)
    across(t, 0)
    greet(0)

    tri = (
        lax.broadcasted_iota(I32, (128, 128), 0) <= lax.broadcasted_iota(I32, (128, 128), 1)
    ).astype(BF16)
    carry = jnp.zeros((32, 1), F32)
    for b in range(rows // 128):
        ids = tenant[:, b * 128:(b + 1) * 128]
        member = (lax.broadcasted_iota(I32, (32, 128), 0) == ids).astype(F32)
        count = carry + jnp.dot(member.astype(BF16), tri, preferred_element_type=F32)
        carry = count[:, 127:128]
        slot = jnp.sum(count * member, axis=0, keepdims=True) - 1.0
        owner = jnp.zeros((1, 128), F32)
        for i in range(n_tenants):
            owner = jnp.where(ids == i, owner_map[i].astype(F32), owner)
        key = owner * float(SLOTS) + slot
        slot_key[:, b * 128:(b + 1) * 128] = key.astype(I32)
        column = jnp.transpose(jnp.broadcast_to(key, (128, 128))).astype(I32)
        slot_hot[b * 128:(b + 1) * 128, :] = (
            column % SLOTS == lax.broadcasted_iota(I32, (128, 128), 1)
        ).astype(BF16)
        row_owner[b * 128:(b + 1) * 128, :] = column // SLOTS

    for j in range(1, nz):
        dz = Z_ORDER[j]
        block = at_tenant(dz, 0)
        wait_block(block)
        if -4 < dz < 0:
            send_block(block, up)
        if 0 < dz < 3:
            send_block(block, dn)
        across(block, j)
        send_u(block)
        relay(j - LAG)
        if j in (2, 4, 6):
            pl.semaphore_wait(token.at[j // 2 - 1], 2)
            if j < 6:
                greet(j // 2)
    for j in range(nz - LAG, nz):
        relay(j)
    for j in range(nz):
        for dx in (1, -1, 2):
            if j < RELAYED and dx == (-1 if j % 2 == 0 else 1):
                continue
            block = at_tenant(Z_ORDER[j], dx)
            wait_block(block)
            send_u(block)

    pick = (
        slot_key[...] == t * SLOTS + lax.broadcasted_iota(I32, (SLOTS, rows), 0)
    ).astype(BF16)
    picked = jnp.dot(pick, g[...], preferred_element_type=F32).astype(BF16)
    part = jnp.transpose(jnp.dot(picked, vq[...], preferred_element_type=F32)).astype(BF16)
    for i in range(n_tensor):
        rank_out[i % NC, i // NC * rank_local:(i // NC + 1) * rank_local, :] = (
            part[i * rank_local:(i + 1) * rank_local, :]
        )
    to_sibling = remote(rank_out.at[1 - c], rank_sib, q_send, q_recv, (t, sibling))
    to_sibling.start()
    to_sibling.wait()
    rank_sum[...] = (rank_out[c].astype(F32) + rank_sib[...].astype(F32)).astype(BF16)

    def ranks_at(i):
        return pl.ds(pl.multiple_of(i * rank_local, rank_local), rank_local)

    for dy in Y_FAR_FIRST:
        to = (y + dy + ny) % ny
        remote(
            rank_sum.at[ranks_at(to)], rank_in.at[ranks_at(y)], r_send, r_recv, (t, at_tensor(dy))
        ).start()
    rank_in[ranks_at(y), :] = rank_sum[ranks_at(y), :]

    step = NC * rows_s

    def shared(i, carry):
        here = pl.ds(pl.multiple_of(i * 2 * step, 2 * step), 2 * step)
        acc[here, :] = jnp.dot(g[here, :], w[...], preferred_element_type=F32)
        return carry

    lax.fori_loop(0, ny // 2, shared, 0)

    wait_bytes(rank_in.at[pl.ds(0, (ny - 1) * rank_local)], r_recv)
    total = jnp.zeros((rank_local, SLOTS), F32)
    for i in range(ny):
        total = total + rank_in[i * rank_local:(i + 1) * rank_local, :].astype(F32)
    code[...] = total.astype(BF16)
    for dz, dx in T_FAR_FIRST:
        remote(code, codes.at[ranks_at(t)], c_send, c_recv, (at_tenant(dz, dx), s)).start()
    codes[ranks_at(t), :] = code[...]
    ur[ranks_at(t), :] = uq[t]

    others = pl.ds(0, (n_tenant - 1) * rank_local)
    wait_bytes(codes.at[others], c_recv)
    wait_bytes(ur.at[others], u_recv)

    owner_lane = lax.broadcasted_iota(I32, (step, n_tenant * rank_local), 1) // rank_local

    def terms(dy):
        d = (y + dy + ny) % ny
        here = pl.ds(pl.multiple_of(d * step, step), step)
        spread_codes = lax.dot_general(
            slot_hot[here, :], codes[...], (((1,), (1,)), ((), ())), preferred_element_type=F32
        )
        owner = row_owner[here, :]
        owner = jnp.concatenate([owner] * (n_tenant * rank_local // 128), axis=1)
        spread_codes = jnp.where(owner == owner_lane, spread_codes, 0.0).astype(BF16)
        acc[here, :] = acc[here, :] + jnp.dot(spread_codes, ur[...], preferred_element_type=F32)
        theirs = pl.ds(pl.multiple_of(d * step + (1 - c) * rows_s, rows_s), rows_s)
        sib_out[d] = acc[theirs, :].astype(BF16)
        remote(sib_out.at[d], sib_in.at[d], x_send, x_recv.at[d], (t, sibling)).start()

    def sibling_ready(dy):
        d = (y + dy + ny) % ny
        wait_bytes(sib_in.at[d], x_recv.at[d])

    pieces = rows_s // PIECE
    low, high = range(pieces // 2), range(pieces // 2, pieces)

    def chip_sum(dy, p):
        d = (y + dy + ny) % ny
        here = pl.ds(pl.multiple_of(d * step + c * rows_s + p * PIECE, PIECE), PIECE)
        return acc[here, :] + sib_in[d, p * PIECE:(p + 1) * PIECE, :].astype(F32)

    def lines(h, p):
        return pl.ds(h * rows_s + p * PIECE, PIECE)

    def ring(way):
        return (ring_up, up_send, up_recv, (t, y_up)) if way > 0 else (
            ring_dn, dn_send, dn_recv, (t, y_dn)
        )

    def push(way, source, h, p):
        slots, send, recv, to = ring(way)
        remote(source, slots.at[lines(h, p)], send, recv.at[h, p], to).start()

    def fresh(way, p):
        slots = ring(way)[0]
        slots[lines(0, p), :] = chip_sum(3 * way, p).astype(BF16)
        push(way, slots.at[lines(0, p)], 1, p)

    def arrived(way, h, p):
        slots, send, recv, to = ring(way)
        wait_bytes(slots.at[lines(h, p)], recv.at[h, p])
        return slots[lines(h, p), :].astype(F32)

    def forward(way, h, p):
        slots = ring(way)[0]
        slots[lines(h, p), :] = (arrived(way, h, p) + chip_sum((3 - h) * way, p)).astype(BF16)
        push(way, slots.at[lines(h, p)], h + 1, p)

    terms(4)
    terms(3)
    sibling_ready(4)
    for p in range(pieces):
        stage[p * PIECE:(p + 1) * PIECE, :] = chip_sum(4, p).astype(BF16)
        push(1 if p in low else -1, stage.at[pl.ds(p * PIECE, PIECE)], 0, p)
    terms(-3)
    sibling_ready(3)
    for p in high:
        fresh(1, p)
    terms(2)
    sibling_ready(-3)
    for p in low:
        fresh(-1, p)
    terms(-2)
    terms(1)
    for p in range(pieces // 2):
        forward(1, 0, low[p])
        forward(-1, 0, high[p])
    terms(-1)
    sibling_ready(2)
    sibling_ready(-2)
    for p in range(pieces):
        forward(1, 1, (p + pieces // 2) % pieces)
        forward(-1, 1, p)
    terms(0)
    sibling_ready(1)
    sibling_ready(-1)
    for p in range(pieces):
        forward(1, 2, (p + pieces // 2) % pieces)
        forward(-1, 2, p)
    sibling_ready(0)
    for i in range(pieces):
        p = (i // 2 + (i % 2) * (pieces // 2)) % pieces
        out[p * PIECE:(p + 1) * PIECE, :] = (
            arrived(1, 3, p) + arrived(-1, 3, p) + chip_sum(0, p)
        ).astype(BF16)

    wait_bytes(g.at[pl.ds(0, (n_tenant - 1) * rows_t)], a_send)
    wait_bytes(ur.at[others], u_send)
    wait_bytes(rank_in.at[pl.ds(0, (ny - 1) * rank_local)], r_send)
    wait_bytes(codes.at[others], c_send)
    wait_bytes(sib_out, x_send)
    wait_bytes(ring_up.at[pl.ds(0, 3 * rows_s + rows_s // 2)], up_send)
    wait_bytes(ring_dn.at[pl.ds(0, 3 * rows_s + rows_s // 2)], dn_send)


def on_device(
    n_tenant, n_tensor,
    activations, base_weight, v_codes, u_codes, group_bits, v_scale, u_scale, tenant_of, owner_map,
):
    rows_t, depth = activations.shape
    cols = base_weight.shape[1]
    rows = tenant_of.shape[0]
    full_rank = v_codes.shape[2]
    rank_local = u_codes.shape[1]
    rows_s = rows // n_tensor
    ny = n_tensor // NC
    all_ranks = n_tenant * rank_local
    vmem = pl.BlockSpec(memory_space=pltpu.VMEM)
    smem = pl.BlockSpec(memory_space=pltpu.SMEM)
    hbm = pl.BlockSpec(memory_space=pl.ANY)
    dma = pltpu.SemaphoreType.DMA
    pieces = rows_s // PIECE
    return pl.pallas_call(
        functools.partial(kernel, n_tenant=n_tenant, n_tensor=n_tensor),
        out_shape=jax.ShapeDtypeStruct((rows_s, cols), BF16),
        in_specs=[hbm, hbm, hbm, hbm, smem, vmem, vmem, vmem, smem],
        out_specs=vmem,
        scratch_shapes=[
            pltpu.VMEM((rows, depth), BF16),
            pltpu.VMEM((depth, cols), BF16),
            pltpu.VMEM((depth, full_rank), I32),
            pltpu.VMEM(u_codes.shape[1:], I32),
            pltpu.VMEM((n_tenant, rank_local, cols), BF16),
            pltpu.VMEM((depth, full_rank), BF16),
            pltpu.VMEM((all_ranks, cols), BF16),
            pltpu.VMEM((NC, full_rank // NC, SLOTS), BF16),
            pltpu.VMEM((full_rank // NC, SLOTS), BF16),
            pltpu.VMEM((full_rank // NC, SLOTS), BF16),
            pltpu.VMEM((full_rank // NC, SLOTS), BF16),
            pltpu.VMEM((rank_local, SLOTS), BF16),
            pltpu.VMEM((all_ranks, SLOTS), BF16),
            pltpu.VMEM((rows, SLOTS), BF16),
            pltpu.VMEM((rows, 128), I32),
            pltpu.VMEM((1, rows), I32),
            pltpu.VMEM((rows, cols), F32),
            pltpu.VMEM((ny, rows_s, cols), BF16),
            pltpu.VMEM((ny, rows_s, cols), BF16),
            pltpu.VMEM((rows_s, cols), BF16),
            pltpu.VMEM((4 * rows_s, cols), BF16),
            pltpu.VMEM((4 * rows_s, cols), BF16),
            dma((4,)), dma, dma((n_tenant,)), dma, dma, dma, dma, dma, dma, dma, dma,
            dma, dma((ny,)), dma, dma((4, pieces)), dma, dma((4, pieces)),
            pltpu.SemaphoreType.REGULAR((3,)),
        ],
        compiler_params=pltpu.CompilerParams(
            collective_id=0, has_side_effects=True, vmem_limit_bytes=58 * 1024 * 1024
        ),
        name="up_projection",
    )(
        activations, base_weight, v_codes, u_codes, group_bits, v_scale, u_scale,
        tenant_of.reshape(1, rows), owner_map,
    )


def solution(mesh):
    in_specs = (
        P("tenant", "tensor"),
        P("tensor", "tenant"),
        P("tenant", "tensor", None),
        P("tenant", "tensor", None),
        P("tenant", None),
        P("tenant", None),
        P("tenant", "tensor"),
        P(),
        P(),
    )
    return jax.shard_map(
        functools.partial(on_device, mesh.shape["tenant"], mesh.shape["tensor"]),
        mesh=mesh, in_specs=in_specs, out_specs=P("tensor", "tenant"), check_vma=False,
    )
```

time: 102 us -> 71 us (0.70)
  the two profiles are of different devices: /device:TPU:8 before, /device:TPU:1 now
where the time goes in v2:
time: 71 us; the launch traced here: 70.9 us
  Pallas kernels  69.2 us (97%)
  local copies, waits for them, and re-layouts  1.6 us (2%)
    pallas_call x1, Pallas kernels, on_device(): pl.pallas_call(functools.partial(kernel, n_tenant=n_tenant, n_tensor=n_te...  69.2 us
    unnamed x1, local copies, waits for them, and re-layouts  1.6 us

profile of v2, /device:TPU:1, one launch (start us, length us, event | category | flops | bytes accessed | tf_op | source)
XLA Modules:
  0.0 70.9 jit_solution(84123169672652681)
XLA Ops:
  0.0 69.2 %up_projection.1 = bf16[96,896]{1,0:T(8,128)(2,1)} custom-call(bf16[48,512]{1,0:T(8,128)(2,1)} %act.1, bf16[512,896]{1,0:T(8,128)(2,1)} %w_hbm.1, s32[1,512,256]{2,1,0:T(8,128)} %vc_hbm.1, s32[1,16,28672]{2,1,0:T(8,128)} %uc_hbm.1, s32[1,8]{1,0:T(1,128)} %bits.1, f32[1,256]{1,0:T(1,128)} %v_scale.1, f32[1,16]{1,0:T(1,128)} %u_scale.1, s32[1,1536]{1,0:T(1,128)} %bitcast.1, ...), custom_call_target="tpu_custom_call" | custom-call | tf_op jit(solution)/shard_map/up_projection/pallas_call | solution.py:357
  69.3 1.6 %copy.11 = bf16[96,896]{1,0:T(8,128)(2,1)} copy(bf16[96,896]{1,0:T(8,128)(2,1)} %up_projection.1) | data formatting | bytes 344064

commit v3 on v2

v3 whole, which is shorter than its diff:
```python
import functools
from typing import Any, NamedTuple

import jax
import jax.numpy as jnp
from jax import lax
from jax.experimental import pallas as pl
from jax.experimental.pallas import tpu as pltpu
from jax.sharding import PartitionSpec as P

MESH = pl.DeviceIdType.MESH
BF16, F32, I32 = jnp.bfloat16, jnp.float32, jnp.int32

NX, NC = 4, 2
SLOTS = 128
Z_ORDER = (0, -1, 1, -2, 2, -3, 3, -4)
RELAYED = 6
PLANES_AFTER = ((), (), (), (), (1, -1, 2, -2), (3, -3, 4), (), ())
SPREAD_FIRST = (0,1,-1)
SPREAD_EARLY, SPREAD_LATE = (2,-2,3,-3),(4,)
LAG = 3
PIECE = 48
STRAIGHT_EARLY = 12
PART_ORDER = (0,2,1,0,1,0,1,0,1,0,1)
Y_FAR_FIRST = (4, 3, -3, 2, -2, 1, -1)
T_MIXED = tuple(
    ((0, 4, 1, -1, 3, -3, 2, -2)[i * 3 % 8], (0, 2, 1, -1)[(i + i // 8) % 4]) for i in range(1, 32)
)
T_FAR_FIRST = tuple(
    sorted(
        ((dz, dx) for dz in Z_ORDER for dx in (0, 1, -1, 2) if (dz, dx) != (0, 0)),
        key=lambda at: -abs(at[0]) - abs(at[1]),
    )
)


class Part(NamedTuple):
    uq: Any
    ur: Any
    sib_out: Any
    sib_in: Any
    stage: Any
    ring_up: Any
    ring_dn: Any
    u_send: Any
    u_recv: Any
    x_send: Any
    x_recv: Any
    up_send: Any
    up_recv: Any
    dn_send: Any
    dn_recv: Any


def kernel(
    act, w_hbm, vc_hbm, uc_hbm, bits, v_scale, u_scale, tenant, owner_map, out,
    g, w, vc, uc, vq, rank_out, rank_sib, rank_sum, rank_in, code, codes,
    slot_hot, row_owner, slot_key, mixed, acc, uz,
    load_sem, a_send, a_recv, uz_send, uz_recv, q_send, q_recv, r_send, r_recv, c_send, c_recv,
    token, *parts, n_tenant, n_tensor, widths,
):
    parts = [Part(*parts[i::len(widths)]) for i in range(len(widths))]
    starts = [sum(widths[:i]) for i in range(len(widths))]
    first, second = parts
    t, s = lax.axis_index("tenant"), lax.axis_index("tensor")
    nz, ny = n_tenant // NX, n_tensor // NC
    z, x = t // NX, t % NX
    y, c = s // NC, s % NC
    rows_t, depth = act.shape
    rows = g.shape[0]
    cols = w.shape[1]
    rank_local = uc.shape[0]
    full_rank = vc.shape[1]
    n_tenants = owner_map.shape[0]
    group = full_rank // bits.shape[1]
    rows_s = out.shape[0]

    def remote(src, dst, send_sem, recv_sem, device):
        return pltpu.make_async_remote_copy(
            src_ref=src, dst_ref=dst, send_sem=send_sem, recv_sem=recv_sem,
            device_id=device, device_id_type=MESH,
        )

    def wait_bytes(ref, sem):
        pltpu.make_async_copy(ref, ref, sem).wait()

    def at_tenant(dz, dx):
        return ((z + dz + nz) % nz) * NX + (x + dx + NX) % NX

    def at_tensor(dy):
        return ((y + dy + ny) % ny) * NC + c

    up, dn, right, left = at_tenant(1, 0), at_tenant(-1, 0), at_tenant(0, 1), at_tenant(0, -1)
    y_up, y_dn, sibling = at_tensor(1), at_tensor(-1), y * NC + 1 - c

    loads = [
        pltpu.make_async_copy(uc_hbm.at[0], uc, load_sem.at[0]),
        pltpu.make_async_copy(vc_hbm.at[0], vc, load_sem.at[1]),
        pltpu.make_async_copy(w_hbm, w, load_sem.at[2]),
        pltpu.make_async_copy(act, g.at[pl.ds(t * rows_t, rows_t)], load_sem.at[3]),
    ]
    for load in loads:
        load.start()

    barrier = pltpu.get_barrier_semaphore()
    for device in (
        (up, s), (dn, s), (at_tenant(2, 0), s), (at_tenant(-2, 0), s),
        (right, s), (left, s), (t, y_up), (t, y_dn), (t, sibling),
    ):
        pl.semaphore_signal(barrier, 1, device_id=device, device_id_type=MESH)

    pl.semaphore_wait(barrier, 9)

    def g_at(block):
        return g.at[pl.ds(block * rows_t, rows_t)]

    def send_block(block, to):
        remote(g_at(block), g_at(block), a_send, a_recv.at[block], (to, s)).start()

    def wait_block(block):
        wait_bytes(g_at(block), a_recv.at[block])

    def send_planes(dz):
        there = (z + dz + nz) % nz
        remote(
            first.uq.at[pl.ds(there * NX, NX)], uz.at[z], uz_send, uz_recv.at[z], (at_tenant(dz, 0), s)
        ).start()

    def hand_on(dz):
        plane = (z + dz + nz) % nz
        source = uz.at[plane] if dz else first.uq.at[pl.ds(z * NX, NX)]
        if dz:
            wait_bytes(source, uz_recv.at[plane])
        here = ranks_at(plane * NX + x)
        for dx in (2, 1, -1):
            there = (x + dx + NX) % NX
            remote(
                source.at[there], first.ur.at[here], first.u_send, first.u_recv,
                (at_tenant(0, dx), s),
            ).start()
        first.ur[here, :] = source[x]

    def send_columns(dz, dx):
        there = at_tenant(dz, dx)
        remote(
            second.uq.at[there], second.ur.at[ranks_at(t)], second.u_send, second.u_recv,
            (there, s),
        ).start()

    def ranks_at(i):
        return pl.ds(pl.multiple_of(i * rank_local, rank_local), rank_local)

    def across(block, j):
        send_block(block, right)
        send_block(block, left)
        if j >= RELAYED:
            send_block(block, at_tenant(0, 2))

    def relay(j):
        if 0 <= j < RELAYED:
            block = at_tenant(Z_ORDER[j], -1 if j % 2 == 0 else 1)
            wait_block(block)
            send_block(block, right if j % 2 == 0 else left)

    def greet(i):
        for device in ((t, y_up), (t, y_dn)):
            pl.semaphore_signal(token.at[i], 1, device_id=device, device_id_type=MESH)

    for to in (up, dn, at_tenant(2, 0), at_tenant(-2, 0), right, left):
        remote(act, g_at(t), a_send, a_recv.at[t], (to, s)).start()
    greet(0)

    u_spread = (jnp.left_shift(1, bits[0, s * rank_local // group]) - 1).astype(F32)
    diagonal = lax.broadcasted_iota(I32, (rank_local, rank_local), 0) == lax.broadcasted_iota(
        I32, (rank_local, rank_local), 1
    )
    u_factor = (
        jnp.sum(jnp.where(diagonal, u_scale[...], 0.0), axis=1, keepdims=True) / u_spread
    )
    loads[0].wait()

    def dequantize_u(i, carry):
        for part, start, width in zip(parts, starts, widths):
            block = uc[:, pl.ds(pl.multiple_of(i * cols + start, 128), width)]
            part.uq[i] = ((2.0 * block.astype(F32) - u_spread) * u_factor).astype(BF16)
        return carry

    lax.fori_loop(0, n_tenant, dequantize_u, 0)

    lane = lax.broadcasted_iota(I32, (1, full_rank), 1)
    v_spread = jnp.zeros((1, full_rank), F32)
    for i in range(bits.shape[1]):
        spread = (jnp.left_shift(1, bits[0, i]) - 1).astype(F32)
        v_spread = jnp.where(lane // group == i, spread, v_spread)
    v_factor = v_scale[...] / v_spread
    loads[1].wait()
    vq[...] = ((2.0 * vc[...].astype(F32) - v_spread) * v_factor).astype(BF16)

    tri = (
        lax.broadcasted_iota(I32, (128, 128), 0) <= lax.broadcasted_iota(I32, (128, 128), 1)
    ).astype(BF16)
    carry = jnp.zeros((32, 1), F32)
    for b in range(rows // 128):
        ids = tenant[:, b * 128:(b + 1) * 128]
        member = (lax.broadcasted_iota(I32, (32, 128), 0) == ids).astype(F32)
        count = carry + jnp.dot(member.astype(BF16), tri, preferred_element_type=F32)
        carry = count[:, 127:128]
        slot = jnp.sum(count * member, axis=0, keepdims=True) - 1.0
        owner = jnp.zeros((1, 128), F32)
        for i in range(n_tenants):
            owner = jnp.where(ids == i, owner_map[i].astype(F32), owner)
        key = owner * float(SLOTS) + slot
        slot_key[:, b * 128:(b + 1) * 128] = key.astype(I32)
        column = jnp.transpose(jnp.broadcast_to(key, (128, 128))).astype(I32)
        slot_hot[b * 128:(b + 1) * 128, :] = (
            column % SLOTS == lax.broadcasted_iota(I32, (128, 128), 1)
        ).astype(BF16)
        row_owner[b * 128:(b + 1) * 128, :] = column // SLOTS

    for j in range(1, nz):
        dz = Z_ORDER[j]
        block = at_tenant(dz, 0)
        wait_block(block)
        if dz == -2:
            send_block(block, up)
            send_block(block, at_tenant(2, 0))
        if dz == 2:
            send_block(block, dn)
        across(block, j)
        relay(j - LAG)
        if j in (2, 4, 6):
            pl.semaphore_wait(token.at[j // 2 - 1], 2)
            if j < 6:
                greet(j // 2)
        for dz in PLANES_AFTER[j]:
            send_planes(dz)
    for j in range(nz - LAG, nz):
        relay(j)
    for j in range(nz):
        for dx in (1, -1, 2):
            if j < RELAYED and dx == (-1 if j % 2 == 0 else 1):
                continue
            block = at_tenant(Z_ORDER[j], dx)
            wait_block(block)
    loads[2].wait()
    loads[3].wait()

    pick = (
        slot_key[...] == t * SLOTS + lax.broadcasted_iota(I32, (SLOTS, rows), 0)
    ).astype(BF16)
    picked = jnp.dot(pick, g[...], preferred_element_type=F32).astype(BF16)
    part = jnp.transpose(jnp.dot(picked, vq[...], preferred_element_type=F32)).astype(BF16)
    for i in range(n_tensor):
        rank_out[i % NC, i // NC * rank_local:(i // NC + 1) * rank_local, :] = (
            part[i * rank_local:(i + 1) * rank_local, :]
        )
    to_sibling = remote(rank_out.at[1 - c], rank_sib, q_send, q_recv, (t, sibling))
    to_sibling.start()
    to_sibling.wait()
    rank_sum[...] = (rank_out[c].astype(F32) + rank_sib[...].astype(F32)).astype(BF16)

    for dy in Y_FAR_FIRST:
        to = (y + dy + ny) % ny
        remote(
            rank_sum.at[ranks_at(to)], rank_in.at[ranks_at(y)], r_send, r_recv, (t, at_tensor(dy))
        ).start()
    rank_in[ranks_at(y), :] = rank_sum[ranks_at(y), :]

    for dz in SPREAD_FIRST:
        hand_on(dz)
    for dz, dx in T_MIXED[:STRAIGHT_EARLY]:
        send_columns(dz, dx)
    step = NC * rows_s

    def shared(i, carry):
        here = pl.ds(pl.multiple_of(i * 2 * step, 2 * step), 2 * step)
        acc[here, :] = jnp.dot(g[here, :], w[...], preferred_element_type=F32)
        return carry

    lax.fori_loop(0, ny // 2, shared, 0)

    for dz in SPREAD_EARLY:
        hand_on(dz)
    wait_bytes(rank_in.at[pl.ds(0, (ny - 1) * rank_local)], r_recv)
    total = jnp.zeros((rank_local, SLOTS), F32)
    for i in range(ny):
        total = total + rank_in[i * rank_local:(i + 1) * rank_local, :].astype(F32)
    code[...] = total.astype(BF16)
    for dz, dx in T_FAR_FIRST:
        remote(code, codes.at[ranks_at(t)], c_send, c_recv, (at_tenant(dz, dx), s)).start()
    codes[ranks_at(t), :] = code[...]
    for dz in SPREAD_LATE:
        hand_on(dz)
    for dz, dx in T_MIXED[STRAIGHT_EARLY:]:
        send_columns(dz, dx)
    second.ur[ranks_at(t), :] = second.uq[t]

    others = pl.ds(0, (n_tenant - 1) * rank_local)
    wait_bytes(codes.at[others], c_recv)
    wait_bytes(first.ur.at[pl.ds(0, nz * (NX - 1) * rank_local)], first.u_recv)

    owner_lane = lax.broadcasted_iota(I32, (step, n_tenant * rank_local), 1) // rank_local

    def mix(dy):
        d = (y + dy + ny) % ny
        here = pl.ds(pl.multiple_of(d * step, step), step)
        spread_codes = lax.dot_general(
            slot_hot[here, :], codes[...], (((1,), (1,)), ((), ())), preferred_element_type=F32
        )
        owner = row_owner[here, :]
        owner = jnp.concatenate([owner] * (n_tenant * rank_local // 128), axis=1)
        mixed[here, :] = jnp.where(owner == owner_lane, spread_codes, 0.0).astype(BF16)

    pieces = rows_s // PIECE
    low, high = range(pieces // 2), range(pieces // 2, pieces)

    def reduce_part(part, start, width):
        span = slice(start, start + width)

        def terms(dy):
            d = (y + dy + ny) % ny
            here = pl.ds(pl.multiple_of(d * step, step), step)
            if part is first:
                mix(dy)
            acc[here, span] = acc[here, span] + jnp.dot(
                mixed[here, :], part.ur[...], preferred_element_type=F32
            )
            theirs = pl.ds(pl.multiple_of(d * step + (1 - c) * rows_s, rows_s), rows_s)
            part.sib_out[d] = acc[theirs, span].astype(BF16)
            remote(
                part.sib_out.at[d], part.sib_in.at[d], part.x_send, part.x_recv.at[d], (t, sibling)
            ).start()

        def sibling_ready(dy):
            d = (y + dy + ny) % ny
            wait_bytes(part.sib_in.at[d], part.x_recv.at[d])

        def chip_sum(dy, p):
            d = (y + dy + ny) % ny
            here = pl.ds(pl.multiple_of(d * step + c * rows_s + p * PIECE, PIECE), PIECE)
            return acc[here, span] + part.sib_in[d, p * PIECE:(p + 1) * PIECE, :].astype(F32)

        def lines(h, p):
            return pl.ds(h * rows_s + p * PIECE, PIECE)

        def ring(way):
            return (part.ring_up, part.up_send, part.up_recv, (t, y_up)) if way > 0 else (
                part.ring_dn, part.dn_send, part.dn_recv, (t, y_dn)
            )

        def push(way, source, h, p):
            slots, send, recv, to = ring(way)
            remote(source, slots.at[lines(h, p)], send, recv.at[h, p], to).start()

        def fresh(way, p):
            slots = ring(way)[0]
            slots[lines(0, p), :] = chip_sum(3 * way, p).astype(BF16)
            push(way, slots.at[lines(0, p)], 1, p)

        def arrived(way, h, p):
            slots, send, recv, to = ring(way)
            wait_bytes(slots.at[lines(h, p)], recv.at[h, p])
            return slots[lines(h, p), :].astype(F32)

        def forward(way, h, p):
            slots = ring(way)[0]
            slots[lines(h, p), :] = (arrived(way, h, p) + chip_sum((3 - h) * way, p)).astype(BF16)
            push(way, slots.at[lines(h, p)], h + 1, p)

        terms(4)
        terms(3)
        sibling_ready(4)
        for p in range(pieces):
            part.stage[p * PIECE:(p + 1) * PIECE, :] = chip_sum(4, p).astype(BF16)
            push(1 if p in low else -1, part.stage.at[pl.ds(p * PIECE, PIECE)], 0, p)
        terms(-3)
        sibling_ready(3)
        for p in high:
            fresh(1, p)
        terms(2)
        sibling_ready(-3)
        for p in low:
            fresh(-1, p)
        terms(-2)
        terms(1)
        yield
        for p in range(pieces // 2):
            forward(1, 0, low[p])
            forward(-1, 0, high[p])
        terms(-1)
        sibling_ready(2)
        sibling_ready(-2)
        yield
        for p in range(pieces):
            forward(1, 1, (p + pieces // 2) % pieces)
            forward(-1, 1, p)
        terms(0)
        sibling_ready(1)
        sibling_ready(-1)
        yield
        for p in range(pieces):
            forward(1, 2, (p + pieces // 2) % pieces)
            forward(-1, 2, p)
        sibling_ready(0)
        yield
        for i in range(pieces):
            p = (i // 2 + (i % 2) * (pieces // 2)) % pieces
            out[p * PIECE:(p + 1) * PIECE, span] = (
                arrived(1, 3, p) + arrived(-1, 3, p) + chip_sum(0, p)
            ).astype(BF16)
        yield

    sums = [reduce_part(*each) for each in zip(parts, starts, widths)]
    for which in PART_ORDER:
        if which == 2:
            wait_bytes(second.ur.at[others], second.u_recv)
            continue
        next(sums[which])

    wait_bytes(g.at[pl.ds(0, (n_tenant - 1) * rows_t)], a_send)
    wait_bytes(uz.at[pl.ds(0, nz - 1)], uz_send)
    wait_bytes(first.ur.at[pl.ds(0, nz * (NX - 1) * rank_local)], first.u_send)
    wait_bytes(second.ur.at[others], second.u_send)
    wait_bytes(rank_in.at[pl.ds(0, (ny - 1) * rank_local)], r_send)
    wait_bytes(codes.at[others], c_send)
    for part in parts:
        wait_bytes(part.sib_out, part.x_send)
        wait_bytes(part.ring_up.at[pl.ds(0, 3 * rows_s + rows_s // 2)], part.up_send)
        wait_bytes(part.ring_dn.at[pl.ds(0, 3 * rows_s + rows_s // 2)], part.dn_send)


def on_device(
    n_tenant, n_tensor,
    activations, base_weight, v_codes, u_codes, group_bits, v_scale, u_scale, tenant_of, owner_map,
):
    rows_t, depth = activations.shape
    cols = base_weight.shape[1]
    rows = tenant_of.shape[0]
    full_rank = v_codes.shape[2]
    rank_local = u_codes.shape[1]
    rows_s = rows // n_tensor
    ny = n_tensor // NC
    all_ranks = n_tenant * rank_local
    vmem = pl.BlockSpec(memory_space=pltpu.VMEM)
    smem = pl.BlockSpec(memory_space=pltpu.SMEM)
    hbm = pl.BlockSpec(memory_space=pl.ANY)
    dma = pltpu.SemaphoreType.DMA
    pieces = rows_s // PIECE
    widths = (cols // 256 * 128 + 128, cols - cols // 256 * 128 - 128)
    return pl.pallas_call(
        functools.partial(kernel, n_tenant=n_tenant, n_tensor=n_tensor, widths=widths),
        out_shape=jax.ShapeDtypeStruct((rows_s, cols), BF16),
        in_specs=[hbm, hbm, hbm, hbm, smem, vmem, vmem, vmem, smem],
        out_specs=vmem,
        scratch_shapes=[
            pltpu.VMEM((rows, depth), BF16),
            pltpu.VMEM((depth, cols), BF16),
            pltpu.VMEM((depth, full_rank), I32),
            pltpu.VMEM(u_codes.shape[1:], I32),
            pltpu.VMEM((depth, full_rank), BF16),
            pltpu.VMEM((NC, full_rank // NC, SLOTS), BF16),
            pltpu.VMEM((full_rank // NC, SLOTS), BF16),
            pltpu.VMEM((full_rank // NC, SLOTS), BF16),
            pltpu.VMEM((full_rank // NC, SLOTS), BF16),
            pltpu.VMEM((rank_local, SLOTS), BF16),
            pltpu.VMEM((all_ranks, SLOTS), BF16),
            pltpu.VMEM((rows, SLOTS), BF16),
            pltpu.VMEM((rows, 128), I32),
            pltpu.VMEM((1, rows), I32),
            pltpu.VMEM((rows, all_ranks), BF16),
            pltpu.VMEM((rows, cols), F32),
            pltpu.VMEM((n_tenant // NX, NX, rank_local, widths[0]), BF16),
            dma((4,)), dma, dma((n_tenant,)), dma, dma((n_tenant // NX,)), dma, dma, dma, dma,
            dma, dma, pltpu.SemaphoreType.REGULAR((3,)),
            *[pltpu.VMEM((n_tenant, rank_local, width), BF16) for width in widths],
            *[pltpu.VMEM((all_ranks, width), BF16) for width in widths],
            *[pltpu.VMEM((ny, rows_s, width), BF16) for width in widths],
            *[pltpu.VMEM((ny, rows_s, width), BF16) for width in widths],
            *[pltpu.VMEM((rows_s, width), BF16) for width in widths],
            *[pltpu.VMEM((4 * rows_s, width), BF16) for width in widths],
            *[pltpu.VMEM((4 * rows_s, width), BF16) for width in widths],
            dma, dma, dma, dma, dma, dma, dma((ny,)), dma((ny,)),
            dma, dma, dma((4, pieces)), dma((4, pieces)),
            dma, dma, dma((4, pieces)), dma((4, pieces)),
        ],
        compiler_params=pltpu.CompilerParams(
            collective_id=0, has_side_effects=True, vmem_limit_bytes=58 * 1024 * 1024
        ),
        name="up_projection",
    )(
        activations, base_weight, v_codes, u_codes, group_bits, v_scale, u_scale,
        tenant_of.reshape(1, rows), owner_map,
    )


def solution(mesh):
    in_specs = (
        P("tenant", "tensor"),
        P("tensor", "tenant"),
        P("tenant", "tensor", None),
        P("tenant", "tensor", None),
        P("tenant", None),
        P("tenant", None),
        P("tenant", "tensor"),
        P(),
        P(),
    )
    return jax.shard_map(
        functools.partial(on_device, mesh.shape["tenant"], mesh.shape["tensor"]),
        mesh=mesh, in_specs=in_specs, out_specs=P("tensor", "tenant"), check_vma=False,
    )
```

time: 71 us -> 69.1 us (0.973)
  Pallas kernels: 69.2 us -> 67.4 us
    pallas_call x1, Pallas kernels: 69.2 us -> 67.4 us  [on_device(): pl.pallas_call(functools.partial(kernel, n_tenant=n_tenant, n_tensor=n_te...]
where the time goes in v3:
time: 69.1 us; the launch traced here: 69 us
  Pallas kernels  67.4 us (98%)
  local copies, waits for them, and re-layouts  1.6 us (2%)
    pallas_call x1, Pallas kernels, on_device(): pl.pallas_call(functools.partial(kernel, n_tenant=n_tenant, n_tensor=n_te...  67.4 us
    unnamed x1, local copies, waits for them, and re-layouts  1.6 us

profile of v3, /device:TPU:1, one launch (start us, length us, event | category | flops | bytes accessed | tf_op | source)
XLA Modules:
  0.0 69.0 jit_solution(12994477991166628995)
XLA Ops:
  0.0 67.4 %up_projection.1 = bf16[96,896]{1,0:T(8,128)(2,1)} custom-call(bf16[48,512]{1,0:T(8,128)(2,1)} %act.1, bf16[512,896]{1,0:T(8,128)(2,1)} %w_hbm.1, s32[1,512,256]{2,1,0:T(8,128)} %vc_hbm.1, s32[1,16,28672]{2,1,0:T(8,128)} %uc_hbm.1, s32[1,8]{1,0:T(1,128)} %bits.1, f32[1,256]{1,0:T(1,128)} %v_scale.1, f32[1,16]{1,0:T(1,128)} %u_scale.1, s32[1,1536]{1,0:T(1,128)} %bitcast.1, ...), custom_call_target="tpu_custom_call" | custom-call | tf_op jit(solution)/shard_map/up_projection/pallas_call | solution.py:450
  67.4 1.6 %copy.11 = bf16[96,896]{1,0:T(8,128)(2,1)} copy(bf16[96,896]{1,0:T(8,128)(2,1)} %up_projection.1) | data formatting | bytes 344064

commit v4 on v3

--- a/solution.py
+++ b/solution.py
@@ -19,6 +19,7 @@
 SPREAD_FIRST = (0,1,-1)
 SPREAD_EARLY, SPREAD_LATE = (2,-2,3,-3),(4,)
 LAG = 3
+MIXED_FIRST = (4, 3, -3, 2)
 PIECE = 48
 STRAIGHT_EARLY = 12
 PART_ORDER = (0,2,1,0,1,0,1,0,1,0,1)
@@ -297,7 +298,6 @@
 
     others = pl.ds(0, (n_tenant - 1) * rank_local)
     wait_bytes(codes.at[others], c_recv)
-    wait_bytes(first.ur.at[pl.ds(0, nz * (NX - 1) * rank_local)], first.u_recv)
 
     owner_lane = lax.broadcasted_iota(I32, (step, n_tenant * rank_local), 1) // rank_local
 
@@ -311,6 +311,10 @@
         owner = jnp.concatenate([owner] * (n_tenant * rank_local // 128), axis=1)
         mixed[here, :] = jnp.where(owner == owner_lane, spread_codes, 0.0).astype(BF16)
 
+    for dy in MIXED_FIRST:
+        mix(dy)
+    wait_bytes(first.ur.at[pl.ds(0, nz * (NX - 1) * rank_local)], first.u_recv)
+
     pieces = rows_s // PIECE
     low, high = range(pieces // 2), range(pieces // 2, pieces)
 
@@ -320,7 +324,7 @@
         def terms(dy):
             d = (y + dy + ny) % ny
             here = pl.ds(pl.multiple_of(d * step, step), step)
-            if part is first:
+            if part is first and dy not in MIXED_FIRST:
                 mix(dy)
             acc[here, span] = acc[here, span] + jnp.dot(
                 mixed[here, :], part.ur[...], preferred_element_type=F32

time: 69.1 us -> 69 us (level)
  no operation moved by 1% of the time
where the time goes in v4:
time: 69 us; the launch traced here: 68.8 us
  Pallas kernels  67.2 us (97%)
  local copies, waits for them, and re-layouts  1.6 us (2%)
    pallas_call x1, Pallas kernels, on_device(): pl.pallas_call(functools.partial(kernel, n_tenant=n_tenant, n_tensor=n_te...  67.2 us
    unnamed x1, local copies, waits for them, and re-layouts  1.6 us

profile of v4, /device:TPU:1, one launch (start us, length us, event | category | flops | bytes accessed | tf_op | source)
XLA Modules:
  0.0 68.8 jit_solution(15632065441339646884)
XLA Ops:
  0.0 67.2 %up_projection.1 = bf16[96,896]{1,0:T(8,128)(2,1)} custom-call(bf16[48,512]{1,0:T(8,128)(2,1)} %act.1, bf16[512,896]{1,0:T(8,128)(2,1)} %w_hbm.1, s32[1,512,256]{2,1,0:T(8,128)} %vc_hbm.1, s32[1,16,28672]{2,1,0:T(8,128)} %uc_hbm.1, s32[1,8]{1,0:T(1,128)} %bits.1, f32[1,256]{1,0:T(1,128)} %v_scale.1, f32[1,16]{1,0:T(1,128)} %u_scale.1, s32[1,1536]{1,0:T(1,128)} %bitcast.1, ...), custom_call_target="tpu_custom_call" | custom-call | tf_op jit(solution)/shard_map/up_projection/pallas_call | solution.py:454
  67.2 1.6 %copy.11 = bf16[96,896]{1,0:T(8,128)(2,1)} copy(bf16[96,896]{1,0:T(8,128)(2,1)} %up_projection.1) | data formatting | bytes 344064
